TPU v7x, 1024 devices: a whole 4x4x32 slice. The times are simulated.
1024 devices in a mesh: dp: 16 (over y, z_hi, core), seq: 64 (over z_lo, x).
Axes of the slice: x: 4, y: 4, z: 32 (z_hi: 2, z_lo: 16; z = z_hi * 16 + z_lo), core: 2. Of those that a mesh axis runs over, the one named last changes fastest.
Arguments:
- qkv_teacher: bfloat16 [16, 3, 16, 512, 768], P('dp', None, None, 'seq'), may hold values from -5.2 to 5.2, as said below
- qkv_student: bfloat16 [16, 3, 16, 512, 768], P('dp', None, None, 'seq'), may hold values from -5.2 to 5.2, as said below
- proto_teacher: bfloat16 [768, 8192], P(None, 'seq'), may hold values from -0.21875 to 0.21875
- proto_student: bfloat16 [768, 8192], P(None, 'seq'), may hold values from -2.25 to 2.25
- center: float32 [8192], P('seq'), may hold values from -9 to 1
- pairing: int32 [16], replicated, may hold values from 0 to 15, as said below
Outputs:
- teacher_out: bfloat16 [16, 16, 512, 768], P('dp', None, 'seq')
- student_out: bfloat16 [16, 16, 512, 768], P('dp', None, 'seq')
- loss: float32 [16], P('dp')
Inputs may be any that keep to these rules, and one draw needn't show every extreme that they name: `qkv_teacher`: random normal values; some positions of the keys may repeat a query's pattern. `qkv_student`: random normal values; some positions of the keys may repeat a query's pattern. pairing[pairing[v]] == v and pairing[v] != v for every view v.
All inputs are finite; a program needn't handle non-finite values.
Results may differ from a plain program's by a relative error of at most 0.001.
The roundings to bfloat16 on the way count: a program that leaves them out, or rounds other values in their place, can miss the bound.
Values may be sent and summed in bfloat16 or wider, within the bound.
A program may use at most 32 MiB of HBM per device.

v0:
```python
import jax
import jax.numpy as jnp
from jax import lax
from jax.sharding import PartitionSpec as P

HD = 64


tau_teacher = 0.07
tau_student = 0.1
norm_eps = 1e-06


def merged_2(value, axis, join):
    pieces = jax.tree.map(lambda part: lax.all_gather(part, axis), value)
    head = jax.tree.map(lambda part: part[0], pieces)
    tail = jax.tree.map(lambda part: part[1:], pieces)
    so_far, _ = lax.scan(lambda so_far, piece: (join(so_far, piece), None), head, tail)
    return so_far


def attend_item(item):
    parts = item.reshape(3, -1, HD)
    scores = lax.dot_general(
        parts[0], parts[1], (((1,), (1,)), ((), ())), preferred_element_type=jnp.float32
    ) * HD ** (-0.5)
    highest = jnp.max(scores, axis=-1, keepdims=True)
    raised = jnp.exp(scores - highest)
    weights = (raised / jnp.sum(raised, axis=-1, keepdims=True)).astype(jnp.bfloat16)
    return (
        jnp.dot(weights, parts[2], preferred_element_type=jnp.float32)
        .astype(jnp.bfloat16)
        .reshape(-1)
    )


def attend_group(grouped):
    return lax.map(attend_item, grouped[0])[None]


def attend_pair(grouped):
    return (attend_group(grouped[0]), attend_group(grouped[1]))


def to_items(qkv_local, nseq):
    frames, pos_dev, width = (qkv_local.shape[2], qkv_local.shape[3], qkv_local.shape[4])
    heads = width // HD
    items = qkv_local[0].reshape(3, frames, pos_dev, heads, HD).transpose(1, 3, 0, 2, 4)
    return items.reshape(nseq, frames * heads // nseq, 3, pos_dev * HD)


def to_token_layout(arrived, frames, pos_dev, heads):
    shaped = arrived.reshape(frames, heads, pos_dev, HD).transpose(0, 2, 1, 3)
    return shaped.reshape(1, frames, pos_dev, heads * HD)


def unit_vector(values):
    return values * lax.rsqrt(jnp.mean(values * values) + norm_eps)


def combine(earlier, later):
    top_teacher = jnp.maximum(earlier[0], later[0])
    first_weight = jnp.exp(earlier[0] - top_teacher)
    second_weight = jnp.exp(later[0] - top_teacher)
    top_student = jnp.maximum(earlier[3], later[3])
    first_share = jnp.exp(earlier[3] - top_student)
    second_share = jnp.exp(later[3] - top_student)
    return (
        top_teacher,
        earlier[1] * first_weight + later[1] * second_weight,
        earlier[2] * first_weight + later[2] * second_weight,
        top_student,
        earlier[4] * first_share + later[4] * second_share,
    )


def local(qkv_teacher, qkv_student, proto_teacher, proto_student, center, pairing):
    nseq = lax.axis_size("seq")
    frames, pos_dev, width = (qkv_teacher.shape[2], qkv_teacher.shape[3], qkv_teacher.shape[4])
    heads = width // HD
    per_dev = frames * heads // nseq
    positions = pos_dev * nseq
    items_teacher = to_items(qkv_teacher, nseq)
    items_student = to_items(qkv_student, nseq)
    frames_teacher, frames_student = attend_pair(
        (
            lax.all_to_all(items_teacher, "seq", split_axis=0, concat_axis=3, tiled=True),
            lax.all_to_all(items_student, "seq", split_axis=0, concat_axis=3, tiled=True),
        )
    )
    sending_teacher = frames_teacher.reshape(1, per_dev, nseq, pos_dev * HD)
    sending_student = frames_student.reshape(1, per_dev, nseq, pos_dev * HD)
    arrived_teacher, arrived_student = (
        lax.all_to_all(sending_teacher, "seq", split_axis=2, concat_axis=0, tiled=True),
        lax.all_to_all(sending_student, "seq", split_axis=2, concat_axis=0, tiled=True),
    )
    teacher_out = to_token_layout(arrived_teacher, frames, pos_dev, heads)
    student_out = to_token_layout(arrived_student, frames, pos_dev, heads)
    scale = 1.0 / (frames * positions)
    pooled_teacher = jnp.sum(teacher_out[0].astype(jnp.float32), axis=(0, 1)) * scale
    pooled_student = jnp.sum(student_out[0].astype(jnp.float32), axis=(0, 1)) * scale
    views = lax.axis_size("dp")
    own_view = lax.axis_index("dp")
    view_ids = jnp.arange(views)
    own_row = (view_ids == own_view).astype(jnp.float32)
    partner = jnp.sum(jnp.where(view_ids == own_view, pairing, 0))
    partner_row = (view_ids == partner).astype(jnp.float32)
    table = own_row[:, None, None] * jnp.stack([pooled_teacher, pooled_student])[None]
    table = lax.psum(table, ("dp", "seq"))
    teacher_pool = jnp.sum(partner_row[:, None] * table[:, 0], axis=0)
    student_pool = jnp.sum(own_row[:, None] * table[:, 1], axis=0)
    logit_teacher = jnp.dot(
        unit_vector(teacher_pool),
        proto_teacher.astype(jnp.float32),
        precision=lax.Precision.HIGHEST,
    )
    logit_student = jnp.dot(
        unit_vector(student_pool),
        proto_student.astype(jnp.float32),
        precision=lax.Precision.HIGHEST,
    )
    sharp = (logit_teacher - center) / tau_teacher
    soft = logit_student / tau_student
    top_teacher = jnp.max(sharp)
    raised = jnp.exp(sharp - top_teacher)
    top_student = jnp.max(soft)
    partials = (
        top_teacher,
        jnp.sum(raised),
        jnp.sum(raised * soft),
        top_student,
        jnp.sum(jnp.exp(soft - top_student)),
    )
    merged = merged_2(partials, "seq", combine)
    loss = merged[3] + jnp.log(merged[4]) - merged[2] / merged[1]
    return (teacher_out, student_out, loss.reshape(1))


def solution(mesh):
    placed = (
        P("dp", None, None, "seq", None),
        P("dp", None, None, "seq", None),
        P(None, "seq"),
        P(None, "seq"),
        P("seq"),
        P(),
    )
    return jax.shard_map(
        local,
        mesh=mesh,
        in_specs=placed,
        out_specs=(P("dp", None, "seq", None), P("dp", None, "seq", None), P("dp")),
        check_vma=False,
    )
```

profile of v0, /device:TPU:24, one launch (start us, length us, event | category | flops | bytes accessed | tf_op | source)
XLA Modules:
  0.0 2434.6 jit_solution(5160460501960440346)
XLA Ops:
  7.2 2.0 reshape_squeeze.7
  9.5 1.7 reshape.102
  11.2 29.5 %all-to-all-start.2 = ((bf16[64,3,3,512]{3,2,1,0:T(4,128)(2,1)}), bf16[64,3,3,512]{3,2,1,0:T(4,128)(2,1)}, u32[]{:S(2)}, u32[]{:S(2)}) async-start(bf16[64,3,3,512]{3,2,1,0:T(4,128)(2,1)} %reshape.102), calls=%async_computation.2 | async-start | bytes 1572864 | tf_op jit(solution)/shard_map/all_to_all | solution.py:88
  42.0 1.7 reshape.99
  43.7 74.6 %all-to-all-done.2 = bf16[64,3,3,512]{3,2,1,0:T(4,128)(2,1)} async-done(((bf16[64,3,3,512]{3,2,1,0:T(4,128)(2,1)}), bf16[64,3,3,512]{3,2,1,0:T(4,128)(2,1)}, u32[]{:S(2)}, u32[]{:S(2)}) %all-to-all-start.2) | async-done | bytes 589856 | tf_op jit(solution)/shard_map/all_to_all | solution.py:88
  118.3 12.7 all-to-all-start
  133.5 17.3 while.39
  136.0 3.3 dynamic_update_slice.10
  141.7 3.3 dynamic_update_slice.10
  147.5 3.3 dynamic_update_slice.10
  150.7 58.2 %all-to-all-done = bf16[64,3,3,512]{3,2,1,0:T(4,128)(2,1)S(1)} async-done(((bf16[64,3,3,512]{3,2,1,0:T(4,128)(2,1)}), bf16[64,3,3,512]{3,2,1,0:T(4,128)(2,1)S(1)}, u32[]{:S(2)}, u32[]{:S(2)}) %all-to-all-start) | async-done | bytes 589856 | tf_op jit(solution)/shard_map/all_to_all | solution.py:87
  208.9 12.7 all-to-all-start.3
  223.0 17.2 while.38
  225.5 3.2 dynamic_update_slice.9
  231.2 3.2 dynamic_update_slice.9
  237.0 3.2 dynamic_update_slice.9
  240.2 16.2 all-to-all-done.3
  256.4 11.4 all-to-all-start.1
  269.0 32.9 %all-to-all-done.1 = bf16[1,3,64,512]{3,1,0,2:T(4,128)(2,1)S(1)} async-done(((bf16[1,3,64,512]{3,1,0,2:T(4,128)(2,1)}), bf16[1,3,64,512]{3,1,0,2:T(4,128)(2,1)S(1)}, u32[]{:S(2)}, u32[]{:S(2)}) %all-to-all-start.1) | async-done | bytes 196640 | tf_op jit(solution)/shard_map/all_to_all | solution.py:94
  307.3 832.3 %all-reduce.8.cloned.1.call-done = f32[16,2,768]{2,0,1:T(8,128)} async-done(((f32[16,2,768]{2,0,1:T(8,128)}), f32[16,2,768]{2,0,1:T(8,128)}) %all-reduce.8.cloned.1.call-update) | async-done | bytes 98320 | tf_op jit(solution)/shard_map/psum | solution.py:109
  1144.3 1.9 exponential_reduce_fusion
  1151.6 1.4 dynamic-update-slice
  1153.0 380.0 %all-reduce.5 = (f32[64]{0:T(128)}, f32[64]{0:T(128)}, f32[64]{0:T(128)}, f32[64]{0:T(128)}, f32[64]{0:T(128)}) all-reduce(f32[64]{0:T(128)S(1)} %dynamic-update-slice, f32[64]{0:T(128)S(1)} %dynamic-update-slice.1, f32[64]{0:T(128)S(1)} %dynamic-update-slice.2, f32[64]{0:T(128)S(1)} %dynamic-update-slice.3, ...), channel_id=1, replica_groups=mesh['dp'=16,'seq'=64] {'seq'}, use_global_device_ids=true, to_apply=%add | all-reduce | flops 320 | bytes 2560
  1536.5 887.6 %while.40 = (s32[]{:T(128)}, f32[]{:T(128)}, f32[]{:T(128)}, f32[]{:T(128)}, f32[]{:T(128)}, /*index=5*/f32[]{:T(128)}, f32[63]{0:T(128)S(1)}, f32[63]{0:T(128)S...) while((s32[]{:T(128)}, f32[]{:T(128)}, f32[]{:T(128)}, f32[]{:T(128)}, ...), condition=%wide.region_22.23_spmd, body=%wide.region_21.22_spmd.sunk | while | flops 17 | bytes 405 | solution.py:18
  (430 shorter events, 248.9 us)
Async XLA Ops:
  7.2 1135.4 %copy-start = (bf16[768,128]{1,0:T(8,128)(2,1)S(1)}, bf16[768,128]{1,0:T(8,128)(2,1)}, u32[]{:S(2)}) copy-start(bf16[768,128]{1,0:T(8,128)(2,1)} %param.15) | copy-start | bytes 589828
  9.5 31.2 %copy-start.1 = (bf16[1,3,16,8,768]{4,3,2,1,0:T(8,128)(2,1)S(1)}, bf16[1,3,16,8,768]{4,3,2,1,0:T(8,128)(2,1)}, u32[]{:S(2)}) copy-start(bf16[1,3,16,8,768]{4,3,2,1,0:T(8,128)(2,1)} %param.12) | copy-start | bytes 1769476
  11.2 107.1 %all-to-all-start.2 = ((bf16[64,3,3,512]{3,2,1,0:T(4,128)(2,1)}), bf16[64,3,3,512]{3,2,1,0:T(4,128)(2,1)}, u32[]{:S(2)}, u32[]{:S(2)}) async-start(bf16[64,3,3,512]{3,2,1,0:T(4,128)(2,1)} %reshape.102), calls=%async_computation.2 | async-start | bytes 1572864 | tf_op jit(solution)/shard_map/all_to_all | solution.py:88
  118.3 90.6 %all-to-all-start = ((bf16[64,3,3,512]{3,2,1,0:T(4,128)(2,1)}), bf16[64,3,3,512]{3,2,1,0:T(4,128)(2,1)S(1)}, u32[]{:S(2)}, u32[]{:S(2)}) async-start(bf16[64,3,3,512]{3,2,1,0:T(4,128)(2,1)} %reshape.99), calls=%async_computation | async-start | bytes 1572864 | tf_op jit(solution)/shard_map/all_to_all | solution.py:87
  208.9 47.5 %all-to-all-start.3 = ((bf16[1,3,64,512]{3,1,0,2:T(4,128)(2,1)}), bf16[1,3,64,512]{3,1,0,2:T(4,128)(2,1)S(1)}, u32[]{:S(2)}, u32[]{:S(2)}) async-start(bf16[1,3,64,512]{3,1,0,2:T(4,128)(2,1)} %bitcast.15), calls=%async_computation.3 | async-start | bytes 524288 | tf_op jit(solution)/shard_map/all_to_all | solution.py:95
  223.0 44.9 %copy-start.4 = (s32[16]{0:T(128)S(1)}, s32[16]{0:T(128)}, u32[]{:S(2)}) copy-start(s32[16]{0:T(128)} %param.17) | copy-start | bytes 196
  256.4 45.5 %all-to-all-start.1 = ((bf16[1,3,64,512]{3,1,0,2:T(4,128)(2,1)}), bf16[1,3,64,512]{3,1,0,2:T(4,128)(2,1)S(1)}, u32[]{:S(2)}, u32[]{:S(2)}) async-start(bf16[1,3,64,512]{3,1,0,2:T(4,128)(2,1)} %bitcast.8), calls=%async_computation.1 | async-start | bytes 524288 | tf_op jit(solution)/shard_map/all_to_all | solution.py:94
  267.8 871.8 %all-reduce.8.cloned.1.call-start = ((), (), s32[]{:S(2)}) async-start(), calls=%async_computation.4 | async-start | bytes 196608 | tf_op jit(solution)/shard_map/psum | solution.py:109
  305.2 838.2 %copy-start.2 = (bf16[768,128]{1,0:T(8,128)(2,1)S(1)}, bf16[768,128]{1,0:T(8,128)(2,1)}, u32[]{:S(2)}) copy-start(bf16[768,128]{1,0:T(8,128)(2,1)} %param.14) | copy-start | bytes 589828
  305.2 838.2 %copy-start.3 = (f32[128]{0:T(128)S(1)}, f32[128]{0:T(128)}, u32[]{:S(2)}) copy-start(f32[128]{0:T(128)} %param.16) | copy-start | bytes 1540
Sparse Core Ops, SparseCore 0:
  303.2 836.3 all-reduce.7
where the time goes:
time: 2440 us; the launch traced here: 2430 us
  waiting for transfers between devices  1010 us (41%)
  loops' own time  678 us (28%)
  blocking collectives  380 us (16%)
  local copies, waits for them, and re-layouts  265 us (11%)
  starting transfers between devices  66.3 us (3%)
    psum x1, waiting for transfers between devices, local(): table = lax.psum(table, ('dp', 'seq'))  832 us
    another operation x1, loops' own time, merged_2(): lax.scan(lambda so_far, piece: (join(so_far, piece), None), head, tail)  677 us
    unnamed x1, blocking collectives  380 us
    dynamic_slice x315, local copies, waits for them, and re-layouts, merged_2(): lax.scan(lambda so_far, piece: (join(so_far, piece), None), head, tail)  210 us
    all_to_all x1, waiting for transfers between devices, local(): lax.all_to_all(items_student, 'seq', split_axis=0, concat_axis=3, tiled=T...  74.6 us
    all_to_all x1, waiting for transfers between devices, local(): lax.all_to_all(items_teacher, 'seq', split_axis=0, concat_axis=3, tiled=T...  58.2 us
  transfers between devices with their start and end apart: 5, of which 5 were waited for; matrix products, arithmetic and copies ran while one was open for 2% of the time, Pallas kernels for 0%

commit v1 on v0

v1 whole, which is shorter than its diff:
```python
import functools
import math

import jax
import jax.numpy as jnp
from jax import lax
from jax.experimental import pallas as pl
from jax.experimental.pallas import tpu as pltpu
from jax.sharding import PartitionSpec as P

HD = 64
NX = 4
PAIRS = 3
LANES = 128

tau_teacher = 0.07
tau_student = 0.1
norm_eps = 1e-06


def spread(step, n):
    return 1 + (n // 2 - 1 + step * (n // 4 if n >= 16 else 1)) % (n - 1)


def drain(ref, sem):
    pltpu.make_async_copy(ref, ref, sem).wait()


def unit_vector(values):
    return values * lax.rsqrt(jnp.mean(values * values) + norm_eps)


def exact_dot(row, matrix):
    high = row.astype(jnp.bfloat16).astype(jnp.float32)
    rest = row - high
    middle = rest.astype(jnp.bfloat16).astype(jnp.float32)
    low = rest - middle
    index = lax.broadcasted_iota(jnp.int32, (8, row.shape[1]), 0)
    parts = jnp.where(index == 0, high, jnp.where(index == 1, middle, jnp.where(index == 2, low, 0.0)))
    products = jnp.dot(parts.astype(jnp.bfloat16), matrix, preferred_element_type=jnp.float32)
    return jnp.sum(products, axis=0, keepdims=True)


def merge(stats):
    lane = lax.broadcasted_iota(jnp.int32, stats.shape, 2)

    def column(i):
        return jnp.sum(jnp.where(lane == i, stats, 0.0), axis=2, keepdims=True)

    top_teacher, top_student = column(0), column(3)
    best_teacher = jnp.max(top_teacher, axis=0, keepdims=True)
    best_student = jnp.max(top_student, axis=0, keepdims=True)
    weight = jnp.exp(top_teacher - best_teacher)
    share = jnp.exp(top_student - best_student)
    return (
        best_teacher[0],
        jnp.sum(column(1) * weight, axis=0),
        jnp.sum(column(2) * weight, axis=0),
        best_student[0],
        jnp.sum(column(4) * share, axis=0),
    )


def packed(values):
    lane = lax.broadcasted_iota(jnp.int32, (1, LANES), 1)
    row = jnp.zeros((1, LANES), jnp.float32)
    for i, value in enumerate(values):
        row = jnp.where(lane == i, value, row)
    return row


def kernel(
    nz, ndp,
    qkv_t, qkv_s, proto_t, proto_s, center, pairing,
    out, loss,
    inp, xb, zb, ob, rb, pool, zpool, mine, xpool, row_t, all_t, stat, zstat, xstat,
    in_sem, x_send, x_recv, z_send, z_recv, rz_send, rz_recv, rx_send, rx_recv, s_send, s_recv,
):
    view = lax.axis_index("dp")
    me = lax.axis_index("seq")
    x = me % NX
    z = me // NX
    width = PAIRS * LANES

    def at_x(d):
        return {"seq": z * NX + (x + d) % NX}

    def at_z(d):
        return {"seq": (z + d) % nz * NX + x}

    def lanes_of(owner, u):
        return pl.ds(pl.multiple_of(owner % 2 * width + u * LANES, LANES), LANES)

    def remote(src, dst, send, recv, where):
        pltpu.make_async_remote_copy(
            src_ref=src, dst_ref=dst, send_sem=send, recv_sem=recv,
            device_id=where, device_id_type=pl.DeviceIdType.MESH,
        ).start()

    def each(n, body):
        lax.fori_loop(0, n, lambda i, c: (body(i), c)[1], 0)

    loads = [
        pltpu.make_async_copy(qkv_t, inp.at[pl.ds(0, 1)], in_sem.at[0]),
        pltpu.make_async_copy(qkv_s, inp.at[pl.ds(1, 1)], in_sem.at[1]),
    ]
    for load in loads:
        load.start()
    barrier = pltpu.get_barrier_semaphore()

    def greet(where):
        pl.semaphore_signal(barrier, inc=1, device_id=where, device_id_type=pl.DeviceIdType.MESH)

    each(nz - 1, lambda i: greet(at_z(i + 1)))
    each(NX - 1, lambda i: greet(at_x(i + 1)))
    each(ndp - 1, lambda i: greet({"dp": (view + i + 1) % ndp}))
    pl.semaphore_wait(barrier, nz - 1 + NX - 1 + ndp - 1)
    for load in loads:
        load.wait()

    def send_x(u):
        for d in range(1, NX):
            owner = (x + d) % NX
            remote(
                inp.at[owner // 2, :, :, :, lanes_of(owner, u)],
                xb.at[u, :, :, NX - 1 - d],
                x_send.at[u], x_recv.at[u], at_x(d),
            )

    def send_own(u):
        def body(i):
            d = spread(i, nz)
            remote(
                inp.at[x // 2, :, (z + d) % nz, :, lanes_of(x, u)],
                zb.at[u, :, z, 0],
                z_send.at[u], z_recv.at[u], at_z(d),
            )

        each(nz - 1, body)
        pltpu.make_async_copy(
            inp.at[x // 2, :, z, :, lanes_of(x, u)], zb.at[u, :, z, 0], z_recv.at[u]
        ).start()

    def send_on(u):
        drain(xb.at[u], x_recv.at[u])

        def body(i):
            d = spread(i, nz)
            remote(
                xb.at[u, :, (z + d) % nz],
                zb.at[u, :, z, pl.ds(1, NX - 1)],
                z_send.at[u], z_recv.at[u], at_z(d),
            )

        each(nz - 1, body)
        pltpu.make_async_copy(
            xb.at[u, :, z], zb.at[u, :, z, pl.ds(1, NX - 1)], z_recv.at[u]
        ).start()

    each(PAIRS, send_x)
    each(PAIRS, send_own)
    each(PAIRS, send_on)

    rows = nz * NX * 8
    block = min(rows, 128)
    rate = HD ** (-0.5) * math.log2(math.e)

    def attend(u):
        drain(zb.at[u], z_recv.at[u])
        flat = lambda ref: ref[...].astype(jnp.float32).reshape(-1, LANES)
        keys = flat(zb.at[u, 1]).astype(jnp.bfloat16)
        values = flat(zb.at[u, 2]).astype(jnp.bfloat16)
        per = block // (NX * 8)
        lane = lax.broadcasted_iota(jnp.int32, (block, LANES), 1)

        def body(i, total):
            query = flat(zb.at[u, 0, pl.ds(i * per, per)])
            halves = []
            for head in range(2):
                own = (lane >= HD) == (head == 1)
                scores = lax.dot_general(
                    jnp.where(own, query, 0.0).astype(jnp.bfloat16), keys,
                    (((1,), (1,)), ((), ())), preferred_element_type=jnp.float32,
                )
                raised = jnp.exp2((scores - jnp.max(scores, axis=1, keepdims=True)) * rate)
                share = 1.0 / jnp.sum(raised, axis=1, keepdims=True)
                halves.append(
                    jnp.dot((raised * share).astype(jnp.bfloat16), values, preferred_element_type=jnp.float32)
                )
            result = jnp.where(lane >= HD, halves[1], halves[0])
            rounded = result.reshape(per, NX, 8, LANES).astype(jnp.bfloat16)
            ob[u, pl.ds(i * per, per)] = rounded
            return total + jnp.sum(
                rounded.astype(jnp.float32).reshape(block, LANES), axis=0, keepdims=True
            )

        pool[u] = lax.fori_loop(0, rows // block, body, jnp.zeros((1, LANES), jnp.float32))

    def send_back(u):
        def body(i):
            d = spread(i, nz)
            remote(ob.at[u, (z + d) % nz], rb.at[u, z], rz_send.at[u], rz_recv.at[u], at_z(d))

        each(nz - 1, body)
        pltpu.make_async_copy(ob.at[u, z], rb.at[u, z], rz_recv.at[u]).start()

    def gather(src, dst, slot, n, where, k):
        def body(i):
            remote(src, dst.at[slot], s_send.at[k], s_recv.at[k], where(i + 1))

        each(n - 1, body)
        pltpu.make_async_copy(src, dst.at[slot], s_recv.at[k]).start()
        drain(dst, s_recv.at[k])

    each(PAIRS - 1, lambda u: (attend(u), send_back(u)))
    attend(PAIRS - 1)
    send_back(PAIRS - 1)

    gather(pool, zpool, z, nz, at_z, 0)
    pool_sum = jnp.sum(zpool[...], axis=0) * (1.0 / (nz * rows))
    mine[...] = pool_sum
    gather(mine, xpool, x, NX, at_x, 1)
    pooled = [
        jnp.concatenate([xpool[2 * s + h, u] for h in range(2) for u in range(PAIRS)], axis=1)
        for s in range(2)
    ]
    sharp = (exact_dot(unit_vector(pooled[0]), proto_t[...]) - center[...]) * (1.0 / tau_teacher)
    soft = exact_dot(unit_vector(pooled[1]), proto_s[...]) * (1.0 / tau_student)
    row_t[...] = sharp
    gather(row_t, all_t, view, ndp, lambda d: {"dp": (view + d) % ndp}, 2)

    def send_home(u):
        drain(rb.at[u], rz_recv.at[u])
        for d in range(1, NX):
            remote(
                rb.at[u, :, d], out.at[x // 2, 0, :, :, lanes_of(x, u)],
                rx_send.at[u], rx_recv, at_x(d),
            )
        pltpu.make_async_copy(
            rb.at[u, :, 0], out.at[x // 2, 0, :, :, lanes_of(x, u)], rx_recv
        ).start()

    each(PAIRS - 1, send_home)

    partner = all_t[pairing[view]]
    top_teacher = jnp.max(partner, axis=1, keepdims=True)
    raised = jnp.exp(partner - top_teacher)
    top_student = jnp.max(soft, axis=1, keepdims=True)
    stat[0] = packed(
        (
            top_teacher,
            jnp.sum(raised, axis=1, keepdims=True),
            jnp.sum(raised * soft, axis=1, keepdims=True),
            top_student,
            jnp.sum(jnp.exp(soft - top_student), axis=1, keepdims=True),
        )
    )
    gather(stat.at[0], zstat, z, nz, at_z, 3)
    stat[1] = packed(merge(zstat[...]))
    send_home(PAIRS - 1)
    gather(stat.at[1], xstat, x, NX, at_x, 4)
    _, total_teacher, product, best_student, total_student = merge(xstat[...])
    value = best_student + jnp.log(total_student) - product / total_teacher
    loss[0] = jnp.sum(value)

    drain(out, rx_recv)

    def finish(u):
        drain(xb.at[u], x_send.at[u])
        drain(zb.at[u, :, pl.ds(0, nz - 1)], z_send.at[u])
        drain(rb.at[u, pl.ds(0, nz - 1)], rz_send.at[u])
        drain(rb.at[u, :, pl.ds(0, NX - 1)], rx_send.at[u])

    each(PAIRS, finish)
    drain(zpool.at[pl.ds(0, nz - 1)], s_send.at[0])
    drain(xpool.at[pl.ds(0, NX - 1)], s_send.at[1])
    drain(all_t.at[pl.ds(0, ndp - 1)], s_send.at[2])
    drain(zstat.at[pl.ds(0, nz - 1)], s_send.at[3])
    drain(xstat.at[pl.ds(0, NX - 1)], s_send.at[4])


def local(nz, ndp, qkv_teacher, qkv_student, proto_teacher, proto_student, center, pairing):
    frames, rows, features = qkv_teacher.shape[2:]
    bf16, f32 = jnp.bfloat16, jnp.float32
    dma = pltpu.SemaphoreType.DMA
    anywhere = pl.BlockSpec(memory_space=pl.ANY)
    vmem = pl.BlockSpec(memory_space=pltpu.VMEM)
    smem = pl.BlockSpec(memory_space=pltpu.SMEM)
    out, loss = pl.pallas_call(
        functools.partial(kernel, nz, ndp),
        out_shape=(
            jax.ShapeDtypeStruct((2, 1, frames, rows, features), bf16),
            jax.ShapeDtypeStruct((1,), f32),
        ),
        in_specs=[anywhere, anywhere, vmem, vmem, vmem, smem],
        out_specs=(anywhere, smem),
        scratch_shapes=[
            pltpu.VMEM((2, 3, frames, rows, features), bf16),
            pltpu.VMEM((PAIRS, 3, nz, NX - 1, rows, LANES), bf16),
            pltpu.VMEM((PAIRS, 3, nz, NX, rows, LANES), bf16),
            pltpu.VMEM((PAIRS, nz, NX, rows, LANES), bf16),
            pltpu.VMEM((PAIRS, nz, NX, rows, LANES), bf16),
            pltpu.VMEM((PAIRS, 1, LANES), f32),
            pltpu.VMEM((nz, PAIRS, 1, LANES), f32),
            pltpu.VMEM((PAIRS, 1, LANES), f32),
            pltpu.VMEM((NX, PAIRS, 1, LANES), f32),
            pltpu.VMEM((1, LANES), f32),
            pltpu.VMEM((ndp, 1, LANES), f32),
            pltpu.VMEM((2, 1, LANES), f32),
            pltpu.VMEM((nz, 1, LANES), f32),
            pltpu.VMEM((NX, 1, LANES), f32),
            dma((2,)),
            dma((PAIRS,)), dma((PAIRS,)),
            dma((PAIRS,)), dma((PAIRS,)),
            dma((PAIRS,)), dma((PAIRS,)),
            dma((PAIRS,)), dma(()),
            dma((5,)), dma((5,)),
        ],
        compiler_params=pltpu.CompilerParams(
            collective_id=0, has_side_effects=True, vmem_limit_bytes=40 * 1024 * 1024
        ),
        name="views",
    )(qkv_teacher, qkv_student, proto_teacher, proto_student, center.reshape(1, -1), pairing)
    return out[0], out[1], loss


def solution(mesh):
    wide = P("dp", None, None, "seq", None)
    return jax.shard_map(
        functools.partial(local, mesh.shape["seq"] // NX, mesh.shape["dp"]),
        mesh=mesh,
        in_specs=(wide, wide, P(None, "seq"), P(None, "seq"), P("seq"), P()),
        out_specs=(P("dp", None, "seq", None), P("dp", None, "seq", None), P("dp")),
        check_vma=False,
    )
```

time: 2440 us -> 218 us (0.09)
  waiting for transfers between devices: 1010 us -> 0 us
  loops' own time: 678 us -> 0 us
  blocking collectives: 380 us -> 0 us
  local copies, waits for them, and re-layouts: 265 us -> 5.4 us
  Pallas kernels: 0 us -> 209 us
  starting transfers between devices: 66.3 us -> 0 us
    psum x1 -> x0, waiting for transfers between devices: 832 us -> none  [local(): table = lax.psum(table, ('dp', 'seq'))]
    another operation x3 -> x0, loops' own time: 678 us -> none  [the longest x1 677 us: merged_2(): lax.scan(lambda so_far, piece: (join(so_far, piece), None), head, tail)]
    unnamed x1 -> x0, blocking collectives: 380 us -> none
    dynamic_slice x315 -> x0, local copies, waits for them, and re-layouts: 210 us -> none  [merged_2(): lax.scan(lambda so_far, piece: (join(so_far, piece), None), head, tail)]
    pallas_call x0 -> x1, Pallas kernels: none -> 209 us  [local(): pl.pallas_call(functools.partial(kernel, nz, ndp), out_shape=(jax.ShapeDt...]
    all_to_all x4 -> x0, waiting for transfers between devices: 182 us -> none  [the longest x1 74.6 us: local(): lax.all_to_all(items_student, 'seq', split_axis=0, concat_axis=3, tiled=T...]
    all_to_all x4 -> x0, starting transfers between devices: 66.3 us -> none  [the longest x1 29.5 us: local(): lax.all_to_all(items_student, 'seq', split_axis=0, concat_axis=3, tiled=T...]
  transfers between devices with their start and end apart: 5 -> 0, of which waited for: 5 -> 0; matrix products, arithmetic and copies ran while one was open for 2% -> 0% of each run, Pallas kernels for 0% -> 0%
where the time goes in v1:
time: 218 us; the launch traced here: 216 us
  Pallas kernels  209 us (96%)
  local copies, waits for them, and re-layouts  5.4 us (2%)
  between operations  2.35 us (1%)
    pallas_call x1, Pallas kernels, local(): pl.pallas_call(functools.partial(kernel, nz, ndp), out_shape=(jax.ShapeDt...  209 us
    unnamed x12, local copies, waits for them, and re-layouts  4.64 us

profile of v1, /device:TPU:24, one launch (start us, length us, event | category | flops | bytes accessed | tf_op | source)
XLA Modules:
  0.0 216.4 jit_solution(7645665482733470576)
XLA Ops:
  0.6 0.0 copy-start.5
  0.6 0.0 copy-start.4
  0.7 0.6 copy-done.5
  1.3 0.0 copy-done.4
  1.3 0.0 copy-start
  1.3 1.1 copy-done
  2.4 0.0 copy-start.1
  2.4 1.1 copy-done.1
  3.4 0.0 copy-start.2
  3.4 0.9 copy-done.2
  4.4 0.0 copy-start.3
  4.4 0.9 copy-done.3
  5.3 208.6 %views.1 = (bf16[2,1,16,8,768]{4,3,2,1,0:T(8,128)(2,1)S(1)}, f32[1]{0:T(128)}) custom-call(bf16[1,3,16,8,768]{4,3,2,1,0:T(8,128)(2,1)S(1)} %copy-done, bf16[1,3,16,8,768]{4,3,2,1,0:T(8,128)(2,1)S(1)} %copy-done.1, bf16[768,128]{1,0:T(8,128)(2,1)S(1)} %copy-done.2, bf16[768,128]{1,0:T(8,128)(2,1)S(1)} %copy-done.3, f32[1,128]{1,0:T(1,128)S(1)} %bitcast.5, ...), custom_call_target="tpu_custom_call" | custom-call | tf_op jit(solution)/shard_map/views/pallas_call | solution.py:289
  213.9 0.8 slice_bitcast_fusion
Async XLA Ops:
  0.6 0.7 copy-start.5
  0.6 0.7 copy-start.4
  1.3 1.1 copy-start
  2.4 1.1 copy-start.1
  3.4 0.9 copy-start.2
  4.4 0.9 copy-start.3

commit v2 on v1

--- a/solution.py
+++ b/solution.py
@@ -10,6 +10,7 @@
 
 HD = 64
 NX = 4
+NH, NC = 2, 2
 PAIRS = 3
 LANES = 128
 
@@ -73,13 +74,16 @@
     nz, ndp,
     qkv_t, qkv_s, proto_t, proto_s, center, pairing,
     out, loss,
-    inp, xb, zb, ob, rb, pool, zpool, mine, xpool, row_t, all_t, stat, zstat, xstat,
-    in_sem, x_send, x_recv, z_send, z_recv, rz_send, rz_recv, rx_send, rx_recv, s_send, s_recv,
+    inp, protos, middle, pairs, xb, zb, ob, hb, pool, zpool, mine, xpool, stat, zstat, xstat,
+    in_sem, x_send, x_recv, z_send, z_recv, h_send, h_recv, o_send, o_recv, s_send, s_recv,
 ):
     view = lax.axis_index("dp")
     me = lax.axis_index("seq")
     x = me % NX
     z = me // NX
+    y, half, core = view // (NH * NC), view // NC % NH, view % NC
+    ring, turn = NH * nz, half * nz + z
+    plane, spot = ndp // NH * NX, (y * NC + core) * NX + x
     width = PAIRS * LANES
 
     def at_x(d):
@@ -87,6 +91,15 @@
 
     def at_z(d):
         return {"seq": (z + d) % nz * NX + x}
+
+    def at_ring(d):
+        to = (turn + d) % ring
+        return {"dp": (y * NH + to // nz) * NC + core, "seq": to % nz * NX + x}
+
+    def at_plane(d):
+        to = (spot + d) % plane
+        row = to // NX
+        return {"dp": (row // NC * NH + half) * NC + row % NC, "seq": z * NX + to % NX}
 
     def lanes_of(owner, u):
         return pl.ds(pl.multiple_of(owner % 2 * width + u * LANES, LANES), LANES)
@@ -97,26 +110,40 @@
             device_id=where, device_id_type=pl.DeviceIdType.MESH,
         ).start()
 
+    def span(first, last, body):
+        lax.fori_loop(first, last, lambda i, c: (body(i), c)[1], 0)
+
     def each(n, body):
-        lax.fori_loop(0, n, lambda i, c: (body(i), c)[1], 0)
-
+        span(0, n, body)
+
+    def far_first(i, n):
+        return 1 + (n // 2 - 1 + i) % (n - 1)
+
+    barrier = pltpu.get_barrier_semaphore()
+
+    def greet(where):
+        pl.semaphore_signal(barrier, inc=1, device_id=where, device_id_type=pl.DeviceIdType.MESH)
+
+    each(ring - 1, lambda i: greet(at_ring(far_first(i, ring))))
+    each(plane - 1, lambda i: greet(at_plane(i + 1)))
     loads = [
-        pltpu.make_async_copy(qkv_t, inp.at[pl.ds(0, 1)], in_sem.at[0]),
-        pltpu.make_async_copy(qkv_s, inp.at[pl.ds(1, 1)], in_sem.at[1]),
+        pltpu.make_async_copy(src, dst, in_sem.at[i])
+        for i, (src, dst) in enumerate(
+            (
+                (qkv_t, inp.at[pl.ds(0, 1)]),
+                (qkv_s, inp.at[pl.ds(1, 1)]),
+                (proto_t, protos.at[0]),
+                (proto_s, protos.at[1]),
+                (center, middle),
+                (pairing, pairs),
+            )
+        )
     ]
     for load in loads:
         load.start()
-    barrier = pltpu.get_barrier_semaphore()
-
-    def greet(where):
-        pl.semaphore_signal(barrier, inc=1, device_id=where, device_id_type=pl.DeviceIdType.MESH)
-
-    each(nz - 1, lambda i: greet(at_z(i + 1)))
-    each(NX - 1, lambda i: greet(at_x(i + 1)))
-    each(ndp - 1, lambda i: greet({"dp": (view + i + 1) % ndp}))
-    pl.semaphore_wait(barrier, nz - 1 + NX - 1 + ndp - 1)
     for load in loads:
         load.wait()
+    pl.semaphore_wait(barrier, ring - 1 + plane - 1)
 
     def send_x(u):
         for d in range(1, NX):
@@ -197,54 +224,69 @@
         pool[u] = lax.fori_loop(0, rows // block, body, jnp.zeros((1, LANES), jnp.float32))
 
     def send_back(u):
+        for d in range(1, NX):
+            remote(
+                ob.at[u, :, d], hb.at[x // 2, :, :, lanes_of(x, u)], h_send.at[u], h_recv.at[u], at_x(d)
+            )
+        pltpu.make_async_copy(
+            ob.at[u, :, 0], hb.at[x // 2, :, :, lanes_of(x, u)], h_recv.at[u]
+        ).start()
+
+    def cut(h, last):
+        first = PAIRS - 1
+        return pl.ds(h * width + (first * LANES if last else 0), LANES if last else first * LANES)
+
+    def send_home(last, begin, end):
         def body(i):
             d = spread(i, nz)
-            remote(ob.at[u, (z + d) % nz], rb.at[u, z], rz_send.at[u], rz_recv.at[u], at_z(d))
-
-        each(nz - 1, body)
-        pltpu.make_async_copy(ob.at[u, z], rb.at[u, z], rz_recv.at[u]).start()
-
-    def gather(src, dst, slot, n, where, k):
-        def body(i):
-            remote(src, dst.at[slot], s_send.at[k], s_recv.at[k], where(i + 1))
-
-        each(n - 1, body)
+            for h in range(2):
+                remote(
+                    hb.at[:, (z + d) % nz, :, cut(h, last)],
+                    out.at[:, 0, z, :, cut(h, last)],
+                    o_send, o_recv, at_z(d),
+                )
+
+        span(begin, end, body)
+
+    def keep_home(last):
+        for h in range(2):
+            pltpu.make_async_copy(hb.at[:, z, :, cut(h, last)], out.at[:, 0, z, :, cut(h, last)], o_recv).start()
+
+    def send_small(src, dst, slot, n, where, k):
+        each(n - 1, lambda i: remote(src, dst.at[slot], s_send.at[k], s_recv.at[k], where(far_first(i, n))))
         pltpu.make_async_copy(src, dst.at[slot], s_recv.at[k]).start()
-        drain(dst, s_recv.at[k])
 
     each(PAIRS - 1, lambda u: (attend(u), send_back(u)))
     attend(PAIRS - 1)
+
+    send_small(pool, zpool, turn, ring, at_ring, 0)
     send_back(PAIRS - 1)
-
-    gather(pool, zpool, z, nz, at_z, 0)
-    pool_sum = jnp.sum(zpool[...], axis=0) * (1.0 / (nz * rows))
-    mine[...] = pool_sum
-    gather(mine, xpool, x, NX, at_x, 1)
+    each(PAIRS - 1, lambda u: drain(ob.at[u], h_recv.at[u]))
+    steps = [nz * k // 16 for k in (0, 6, 10)] + [nz - 1]
+    send_home(False, steps[0], steps[1])
+    keep_home(False)
+    drain(zpool, s_recv.at[0])
+    for h in range(NH):
+        mine[h] = jnp.sum(zpool[pl.ds(h * nz, nz)], axis=0) * (1.0 / (nz * rows))
+    send_small(mine, xpool, spot, plane, at_plane, 1)
+    send_home(False, steps[1], steps[2])
+    drain(xpool, s_recv.at[1])
+
+    partner = pairs[view]
+    wanted = (
+        (partner // (NH * NC) * NC + partner % NC, partner // NC % NH),
+        (y * NC + core, half),
+    )
     pooled = [
-        jnp.concatenate([xpool[2 * s + h, u] for h in range(2) for u in range(PAIRS)], axis=1)
-        for s in range(2)
+        jnp.concatenate(
+            [xpool[row * NX + 2 * s + h, side, u] for h in range(2) for u in range(PAIRS)], axis=1
+        )
+        for s, (row, side) in enumerate(wanted)
     ]
-    sharp = (exact_dot(unit_vector(pooled[0]), proto_t[...]) - center[...]) * (1.0 / tau_teacher)
-    soft = exact_dot(unit_vector(pooled[1]), proto_s[...]) * (1.0 / tau_student)
-    row_t[...] = sharp
-    gather(row_t, all_t, view, ndp, lambda d: {"dp": (view + d) % ndp}, 2)
-
-    def send_home(u):
-        drain(rb.at[u], rz_recv.at[u])
-        for d in range(1, NX):
-            remote(
-                rb.at[u, :, d], out.at[x // 2, 0, :, :, lanes_of(x, u)],
-                rx_send.at[u], rx_recv, at_x(d),
-            )
-        pltpu.make_async_copy(
-            rb.at[u, :, 0], out.at[x // 2, 0, :, :, lanes_of(x, u)], rx_recv
-        ).start()
-
-    each(PAIRS - 1, send_home)
-
-    partner = all_t[pairing[view]]
-    top_teacher = jnp.max(partner, axis=1, keepdims=True)
-    raised = jnp.exp(partner - top_teacher)
+    sharp = (exact_dot(unit_vector(pooled[0]), protos[0]) - middle[...]) * (1.0 / tau_teacher)
+    soft = exact_dot(unit_vector(pooled[1]), protos[1]) * (1.0 / tau_student)
+    top_teacher = jnp.max(sharp, axis=1, keepdims=True)
+    raised = jnp.exp(sharp - top_teacher)
     top_student = jnp.max(soft, axis=1, keepdims=True)
     stat[0] = packed(
         (
@@ -255,28 +297,32 @@
             jnp.sum(jnp.exp(soft - top_student), axis=1, keepdims=True),
         )
     )
-    gather(stat.at[0], zstat, z, nz, at_z, 3)
+    send_small(stat.at[0], zstat, z, nz, at_z, 2)
+    send_home(False, steps[2], steps[3])
+    drain(ob.at[PAIRS - 1], h_recv.at[PAIRS - 1])
+    keep_home(True)
+    send_home(True, 0, steps[1])
+    drain(zstat, s_recv.at[2])
     stat[1] = packed(merge(zstat[...]))
-    send_home(PAIRS - 1)
-    gather(stat.at[1], xstat, x, NX, at_x, 4)
+    send_small(stat.at[1], xstat, x, NX, at_x, 3)
+    send_home(True, steps[1], steps[3])
+    drain(xstat, s_recv.at[3])
     _, total_teacher, product, best_student, total_student = merge(xstat[...])
     value = best_student + jnp.log(total_student) - product / total_teacher
     loss[0] = jnp.sum(value)
 
-    drain(out, rx_recv)
-
     def finish(u):
         drain(xb.at[u], x_send.at[u])
         drain(zb.at[u, :, pl.ds(0, nz - 1)], z_send.at[u])
-        drain(rb.at[u, pl.ds(0, nz - 1)], rz_send.at[u])
-        drain(rb.at[u, :, pl.ds(0, NX - 1)], rx_send.at[u])
+        drain(ob.at[u, :, pl.ds(0, NX - 1)], h_send.at[u])
 
     each(PAIRS, finish)
-    drain(zpool.at[pl.ds(0, nz - 1)], s_send.at[0])
-    drain(xpool.at[pl.ds(0, NX - 1)], s_send.at[1])
-    drain(all_t.at[pl.ds(0, ndp - 1)], s_send.at[2])
-    drain(zstat.at[pl.ds(0, nz - 1)], s_send.at[3])
-    drain(xstat.at[pl.ds(0, NX - 1)], s_send.at[4])
+    drain(zpool.at[pl.ds(0, ring - 1)], s_send.at[0])
+    drain(xpool.at[pl.ds(0, plane - 1)], s_send.at[1])
+    drain(zstat.at[pl.ds(0, nz - 1)], s_send.at[2])
+    drain(xstat.at[pl.ds(0, NX - 1)], s_send.at[3])
+    drain(hb.at[:, pl.ds(0, nz - 1)], o_send)
+    drain(out, o_recv)
 
 
 def local(nz, ndp, qkv_teacher, qkv_student, proto_teacher, proto_student, center, pairing):
@@ -284,7 +330,6 @@
     bf16, f32 = jnp.bfloat16, jnp.float32
     dma = pltpu.SemaphoreType.DMA
     anywhere = pl.BlockSpec(memory_space=pl.ANY)
-    vmem = pl.BlockSpec(memory_space=pltpu.VMEM)
     smem = pl.BlockSpec(memory_space=pltpu.SMEM)
     out, loss = pl.pallas_call(
         functools.partial(kernel, nz, ndp),
@@ -292,32 +337,33 @@
             jax.ShapeDtypeStruct((2, 1, frames, rows, features), bf16),
             jax.ShapeDtypeStruct((1,), f32),
         ),
-        in_specs=[anywhere, anywhere, vmem, vmem, vmem, smem],
+        in_specs=[anywhere] * 6,
         out_specs=(anywhere, smem),
         scratch_shapes=[
             pltpu.VMEM((2, 3, frames, rows, features), bf16),
+            pltpu.VMEM((2, features, LANES), bf16),
+            pltpu.VMEM((1, LANES), f32),
+            pltpu.SMEM((ndp,), jnp.int32),
             pltpu.VMEM((PAIRS, 3, nz, NX - 1, rows, LANES), bf16),
             pltpu.VMEM((PAIRS, 3, nz, NX, rows, LANES), bf16),
             pltpu.VMEM((PAIRS, nz, NX, rows, LANES), bf16),
-            pltpu.VMEM((PAIRS, nz, NX, rows, LANES), bf16),
+            pltpu.VMEM((2, nz, rows, features), bf16),
             pltpu.VMEM((PAIRS, 1, LANES), f32),
-            pltpu.VMEM((nz, PAIRS, 1, LANES), f32),
-            pltpu.VMEM((PAIRS, 1, LANES), f32),
-            pltpu.VMEM((NX, PAIRS, 1, LANES), f32),
-            pltpu.VMEM((1, LANES), f32),
-            pltpu.VMEM((ndp, 1, LANES), f32),
+            pltpu.VMEM((NH * nz, PAIRS, 1, LANES), f32),
+            pltpu.VMEM((NH, PAIRS, 1, LANES), f32),
+            pltpu.VMEM((ndp // NH * NX, NH, PAIRS, 1, LANES), f32),
             pltpu.VMEM((2, 1, LANES), f32),
             pltpu.VMEM((nz, 1, LANES), f32),
             pltpu.VMEM((NX, 1, LANES), f32),
-            dma((2,)),
+            dma((6,)),
             dma((PAIRS,)), dma((PAIRS,)),
             dma((PAIRS,)), dma((PAIRS,)),
             dma((PAIRS,)), dma((PAIRS,)),
-            dma((PAIRS,)), dma(()),
-            dma((5,)), dma((5,)),
+            dma(()), dma(()),
+            dma((4,)), dma((4,)),
         ],
         compiler_params=pltpu.CompilerParams(
-            collective_id=0, has_side_effects=True, vmem_limit_bytes=40 * 1024 * 1024
+            collective_id=0, has_side_effects=True, vmem_limit_bytes=58 * 1024 * 1024
         ),
         name="views",
     )(qkv_teacher, qkv_student, proto_teacher, proto_student, center.reshape(1, -1), pairing)

time: 218 us -> 187 us (0.86)
  Pallas kernels: 209 us -> 182 us
  local copies, waits for them, and re-layouts: 5.4 us -> 1.79 us
    pallas_call x1, Pallas kernels: 209 us -> 182 us  [local(): pl.pallas_call(functools.partial(kernel, nz, ndp), out_shape=(jax.ShapeDt...]
    unnamed x12 -> x0, local copies, waits for them, and re-layouts: 4.64 us -> none
where the time goes in v2:
time: 187 us; the launch traced here: 186 us
  Pallas kernels  182 us (97%)
  between operations  2.46 us (1%)
    pallas_call x1, Pallas kernels, local(): pl.pallas_call(functools.partial(kernel, nz, ndp), out_shape=(jax.ShapeDt...  182 us

profile of v2, /device:TPU:24, one launch (start us, length us, event | category | flops | bytes accessed | tf_op | source)
XLA Modules:
  0.0 186.1 jit_solution(4780519064679254606)
XLA Ops:
  0.6 181.9 %views.1 = (bf16[2,1,16,8,768]{4,3,2,1,0:T(8,128)(2,1)}, f32[1]{0:T(128)}) custom-call(bf16[1,3,16,8,768]{4,3,2,1,0:T(8,128)(2,1)} %qkv_t.1, bf16[1,3,16,8,768]{4,3,2,1,0:T(8,128)(2,1)} %qkv_s.1, bf16[768,128]{1,0:T(8,128)(2,1)} %proto_t.1, bf16[768,128]{1,0:T(8,128)(2,1)} %proto_s.1, f32[1,128]{1,0:T(1,128)} %bitcast.5, s32[16]{0:T(128)} %pairing.1), custom_call_target="tpu_custom_call" | custom-call | tf_op jit(solution)/shard_map/views/pallas_call | solution.py:334
  182.5 1.8 slice_bitcast_fusion

commit v3 on v2

--- a/solution.py
+++ b/solution.py
@@ -74,8 +74,8 @@
     nz, ndp,
     qkv_t, qkv_s, proto_t, proto_s, center, pairing,
     out, loss,
-    inp, protos, middle, pairs, xb, zb, ob, hb, pool, zpool, mine, xpool, stat, zstat, xstat,
-    in_sem, x_send, x_recv, z_send, z_recv, h_send, h_recv, o_send, o_recv, s_send, s_recv,
+    inp, protos, middle, pairs, xb, zb, ob, hb, pool, zpool, mine, xpool, stat, zstat,
+    in_sem, x_send, x_recv, z_send, z_recv, h_send, h_recv, o_send, o_recv, s_send, s_recv, p_send, p_recv,
 ):
     view = lax.axis_index("dp")
     me = lax.axis_index("seq")
@@ -132,9 +132,9 @@
             (
                 (qkv_t, inp.at[pl.ds(0, 1)]),
                 (qkv_s, inp.at[pl.ds(1, 1)]),
-                (proto_t, protos.at[0]),
-                (proto_s, protos.at[1]),
-                (center, middle),
+                (proto_t, protos.at[0, x]),
+                (proto_s, protos.at[1, x]),
+                (center, middle.at[x]),
                 (pairing, pairs),
             )
         )
@@ -186,6 +186,9 @@
 
     each(PAIRS, send_x)
     each(PAIRS, send_own)
+    for d in range(1, NX):
+        remote(protos.at[:, x], protos.at[:, x], p_send.at[0], p_recv.at[0], at_x(d))
+        remote(middle.at[x], middle.at[x], p_send.at[1], p_recv.at[1], at_x(d))
     each(PAIRS, send_on)
 
     rows = nz * NX * 8
@@ -262,14 +265,15 @@
     send_small(pool, zpool, turn, ring, at_ring, 0)
     send_back(PAIRS - 1)
     each(PAIRS - 1, lambda u: drain(ob.at[u], h_recv.at[u]))
-    steps = [nz * k // 16 for k in (0, 6, 10)] + [nz - 1]
-    send_home(False, steps[0], steps[1])
+    send_home(False, 0, nz - 1)
     keep_home(False)
     drain(zpool, s_recv.at[0])
     for h in range(NH):
         mine[h] = jnp.sum(zpool[pl.ds(h * nz, nz)], axis=0) * (1.0 / (nz * rows))
     send_small(mine, xpool, spot, plane, at_plane, 1)
-    send_home(False, steps[1], steps[2])
+    drain(ob.at[PAIRS - 1], h_recv.at[PAIRS - 1])
+    keep_home(True)
+    send_home(True, 0, nz - 1)
     drain(xpool, s_recv.at[1])
 
     partner = pairs[view]
@@ -283,12 +287,21 @@
         )
         for s, (row, side) in enumerate(wanted)
     ]
-    sharp = (exact_dot(unit_vector(pooled[0]), protos[0]) - middle[...]) * (1.0 / tau_teacher)
-    soft = exact_dot(unit_vector(pooled[1]), protos[1]) * (1.0 / tau_student)
+    drain(protos.at[:, pl.ds(0, NX - 1)], p_recv.at[0])
+    drain(middle.at[pl.ds(0, NX - 1)], p_recv.at[1])
+    units = [unit_vector(row) for row in pooled]
+
+    def over_x(parts):
+        return jnp.concatenate([parts(i) for i in range(NX)], axis=1)
+
+    sharp = (over_x(lambda i: exact_dot(units[0], protos[0, i])) - over_x(lambda i: middle[i])) * (
+        1.0 / tau_teacher
+    )
+    soft = over_x(lambda i: exact_dot(units[1], protos[1, i])) * (1.0 / tau_student)
     top_teacher = jnp.max(sharp, axis=1, keepdims=True)
     raised = jnp.exp(sharp - top_teacher)
     top_student = jnp.max(soft, axis=1, keepdims=True)
-    stat[0] = packed(
+    stat[...] = packed(
         (
             top_teacher,
             jnp.sum(raised, axis=1, keepdims=True),
@@ -297,17 +310,9 @@
             jnp.sum(jnp.exp(soft - top_student), axis=1, keepdims=True),
         )
     )
-    send_small(stat.at[0], zstat, z, nz, at_z, 2)
-    send_home(False, steps[2], steps[3])
-    drain(ob.at[PAIRS - 1], h_recv.at[PAIRS - 1])
-    keep_home(True)
-    send_home(True, 0, steps[1])
+    send_small(stat, zstat, z, nz, at_z, 2)
     drain(zstat, s_recv.at[2])
-    stat[1] = packed(merge(zstat[...]))
-    send_small(stat.at[1], xstat, x, NX, at_x, 3)
-    send_home(True, steps[1], steps[3])
-    drain(xstat, s_recv.at[3])
-    _, total_teacher, product, best_student, total_student = merge(xstat[...])
+    _, total_teacher, product, best_student, total_student = merge(zstat[...])
     value = best_student + jnp.log(total_student) - product / total_teacher
     loss[0] = jnp.sum(value)
 
@@ -320,7 +325,8 @@
     drain(zpool.at[pl.ds(0, ring - 1)], s_send.at[0])
     drain(xpool.at[pl.ds(0, plane - 1)], s_send.at[1])
     drain(zstat.at[pl.ds(0, nz - 1)], s_send.at[2])
-    drain(xstat.at[pl.ds(0, NX - 1)], s_send.at[3])
+    drain(protos.at[:, pl.ds(0, NX - 1)], p_send.at[0])
+    drain(middle.at[pl.ds(0, NX - 1)], p_send.at[1])
     drain(hb.at[:, pl.ds(0, nz - 1)], o_send)
     drain(out, o_recv)
 
@@ -341,8 +347,8 @@
         out_specs=(anywhere, smem),
         scratch_shapes=[
             pltpu.VMEM((2, 3, frames, rows, features), bf16),
-            pltpu.VMEM((2, features, LANES), bf16),
-            pltpu.VMEM((1, LANES), f32),
+            pltpu.VMEM((2, NX, features, LANES), bf16),
+            pltpu.VMEM((NX, 1, LANES), f32),
             pltpu.SMEM((ndp,), jnp.int32),
             pltpu.VMEM((PAIRS, 3, nz, NX - 1, rows, LANES), bf16),
             pltpu.VMEM((PAIRS, 3, nz, NX, rows, LANES), bf16),
@@ -352,15 +358,15 @@
             pltpu.VMEM((NH * nz, PAIRS, 1, LANES), f32),
             pltpu.VMEM((NH, PAIRS, 1, LANES), f32),
             pltpu.VMEM((ndp // NH * NX, NH, PAIRS, 1, LANES), f32),
-            pltpu.VMEM((2, 1, LANES), f32),
+            pltpu.VMEM((1, LANES), f32),
             pltpu.VMEM((nz, 1, LANES), f32),
-            pltpu.VMEM((NX, 1, LANES), f32),
             dma((6,)),
             dma((PAIRS,)), dma((PAIRS,)),
             dma((PAIRS,)), dma((PAIRS,)),
             dma((PAIRS,)), dma((PAIRS,)),
             dma(()), dma(()),
-            dma((4,)), dma((4,)),
+            dma((3,)), dma((3,)),
+            dma((2,)), dma((2,)),
         ],
         compiler_params=pltpu.CompilerParams(
             collective_id=0, has_side_effects=True, vmem_limit_bytes=58 * 1024 * 1024

time: 187 us -> 183 us (0.979)
  Pallas kernels: 182 us -> 178 us
    pallas_call x1, Pallas kernels: 182 us -> 178 us  [local(): pl.pallas_call(functools.partial(kernel, nz, ndp), out_shape=(jax.ShapeDt...]
where the time goes in v3:
time: 183 us
  Pallas kernels  178 us (97%)
  between operations  2.46 us (1%)
    pallas_call x1, Pallas kernels, local(): pl.pallas_call(functools.partial(kernel, nz, ndp), out_shape=(jax.ShapeDt...  178 us

profile of v3, /device:TPU:24, one launch (start us, length us, event | category | flops | bytes accessed | tf_op | source)
XLA Modules:
  0.0 182.7 jit_solution(11807096879110861461)
XLA Ops:
  0.6 178.4 %views.1 = (bf16[2,1,16,8,768]{4,3,2,1,0:T(8,128)(2,1)}, f32[1]{0:T(128)}) custom-call(bf16[1,3,16,8,768]{4,3,2,1,0:T(8,128)(2,1)} %qkv_t.1, bf16[1,3,16,8,768]{4,3,2,1,0:T(8,128)(2,1)} %qkv_s.1, bf16[768,128]{1,0:T(8,128)(2,1)} %proto_t.1, bf16[768,128]{1,0:T(8,128)(2,1)} %proto_s.1, f32[1,128]{1,0:T(1,128)} %bitcast.5, s32[16]{0:T(128)} %pairing.1), custom_call_target="tpu_custom_call" | custom-call | tf_op jit(solution)/shard_map/views/pallas_call | solution.py:340
  179.1 1.8 slice_bitcast_fusion
